TPU v7x, 512 devices: a whole 4x4x16 slice. The times are simulated.
512 devices in a mesh: prow: 16 (over x, y), pcol: 32 (over z, core).
Axes of the slice: x: 4, y: 4, z: 16, core: 2. Of those that a mesh axis runs over, the one named last changes fastest.
Arguments:
- a_matrix: float32 [16384, 8192], P('prow', 'pcol'), as said below
- row_perms: int32 [2, 128], replicated, may hold values from 0 to 127, each once within a row
- dest_rows: int32 [2, 128], replicated, may hold values from 0 to 127, as said below
- row_mask: int32 [2, 128], replicated, may hold values 0 or 1
- col_mask: int32 [2, 64], replicated, may hold values 0 or 1
Outputs:
- schur_out: float32 [16384, 8192], P('prow', 'pcol')
- l_panels: float32 [16384, 256], P('prow')
Inputs may be any that keep to these rules, and one draw needn't show every extreme that they name: `a_matrix`: the two leading diagonal blocks of the window carry 16 sqrt(128) on their diagonal, on top of entries of order one. `dest_rows`: for each section, a permutation of the 128 block rows that keeps a block row's position among the 8 block rows of its device; block rows of one device whose positions differ by less than 16 go to different devices.
All inputs are finite; a program needn't handle non-finite values.
Results may differ from a plain program's by a relative error of at most 0.0001.
Values sent between devices are 32-bit elements; how exact they have to be, the bound alone decides.
No kernel may reach another device: no remote copies, remote signals or barrier semaphores. Data moves between devices by JAX's collectives and lax.ppermute only.
A program may use at most 64 MiB of HBM per device.

v0:
```python
import jax
import jax.numpy as jnp
from jax import lax
from jax.sharding import PartitionSpec as P

SWEEPS = 3


def spread(block, axis, owner):
    block = jnp.where(lax.axis_index(axis) == owner, block, jnp.zeros_like(block))
    return lax.psum(block, axis)


def refine(pivot_block):
    width = pivot_block.shape[0]
    identity = jnp.eye(width, dtype=pivot_block.dtype)
    scale = width * (jnp.mean(pivot_block * pivot_block) + 1e-06)
    approx = pivot_block.T / scale
    for sweep in range(SWEEPS):
        inner = jnp.dot(pivot_block, approx, precision=lax.Precision.HIGHEST)
        approx = jnp.dot(approx, 2.0 * identity - inner, precision=lax.Precision.HIGHEST)
    return approx


def block_flags(mask_row, owner, count, section):
    local = lax.dynamic_slice_in_dim(mask_row, owner * count, count)
    global_ids = owner * count + jnp.arange(count, dtype=jnp.int32)
    return ((local == 1) & (global_ids > section)).astype(jnp.float32)


def shards(a_matrix, row_perms, dest_rows, row_mask, col_mask):
    width = row_perms.shape[1]
    rows_here = a_matrix.shape[0] // width
    cols_here = a_matrix.shape[1] // width
    n_owners = lax.axis_size("prow")
    capacity = (rows_here + n_owners - 1) // n_owners
    my_row = lax.axis_index("prow")
    my_col = lax.axis_index("pcol")
    owner_ids = jnp.arange(n_owners, dtype=jnp.int32)
    slot_ids = jnp.arange(rows_here, dtype=jnp.int32)
    slot_group = slot_ids // n_owners
    group_ids = jnp.arange(capacity, dtype=jnp.int32)
    group_map = (slot_group[:, None] == group_ids[None, :]).astype(jnp.float32)
    current = a_matrix
    panels = []
    for section in range(2):
        root_row = section // rows_here
        local_row = section % rows_here
        local_col = section % cols_here
        block = current[local_row * width : (local_row + 1) * width]
        pivoted = jnp.take(block, row_perms[section], axis=0)
        upper = spread(pivoted, "prow", root_row)
        current = current.at[local_row * width : (local_row + 1) * width].set(
            jnp.where(my_row == root_row, upper, block)
        )
        inverse = refine(upper[:, local_col * width : (local_col + 1) * width])
        column = current[:, local_col * width : (local_col + 1) * width]
        row_flags = block_flags(row_mask[section], my_row, rows_here, section)
        lower = jnp.dot(column, inverse, precision=lax.Precision.HIGHEST)
        lower = lower * jnp.repeat(row_flags, width)[:, None]
        gathered = spread(lower, "pcol", section // cols_here)
        panels.append(gathered)
        col_flags = block_flags(col_mask[section], my_col, cols_here, section)
        kept = upper * jnp.repeat(col_flags, width)[None, :]
        targets = lax.dynamic_slice_in_dim(dest_rows[section], my_row * rows_here, rows_here)
        target_dev = targets // rows_here
        send_map = (
            (target_dev[None, None, :] == owner_ids[:, None, None])
            & (slot_group[None, None, :] == group_ids[None, :, None])
        ).astype(jnp.float32)
        mine = my_row * rows_here + slot_ids
        all_targets = dest_rows[section].reshape(n_owners, rows_here)
        matches = (all_targets[None, :, :] == mine[:, None, None]).astype(jnp.float32)
        recv_map = jnp.einsum("tpr,rk->tpk", matches, group_map, precision=lax.Precision.HIGHEST)
        product = jnp.dot(gathered, kept, precision=lax.Precision.HIGHEST)
        outgoing = jnp.einsum(
            "qkr,rbc->qkbc",
            send_map,
            product.reshape(rows_here, width, -1),
            precision=lax.Precision.HIGHEST,
        ).reshape(n_owners * capacity * width, -1)
        arrived = lax.all_to_all(outgoing, "prow", split_axis=0, concat_axis=0, tiled=True).reshape(
            n_owners, capacity, width, -1
        )
        placed = jnp.einsum(
            "tpk,pkbc->tbc", recv_map, arrived, precision=lax.Precision.HIGHEST
        ).reshape(rows_here * width, -1)
        current = current - placed
    return (current, jnp.concatenate(panels, axis=1))


def solution(mesh):
    placed = (P("prow", "pcol"), P(), P(), P(), P())
    return jax.shard_map(
        shards,
        mesh=mesh,
        in_specs=placed,
        out_specs=(P("prow", "pcol"), P("prow", None)),
        check_vma=False,
    )
```

profile of v0, /device:TPU:8, one launch (start us, length us, event | category | flops | bytes accessed | tf_op | source)
XLA Modules:
  0.0 773.6 jit_solution(13413972947805506345)
XLA Ops:
  7.3 1.2 copy.34
  8.5 0.8 gather_fusion
  10.4 118.5 %all-reduce.5.cloned.1.call-done = f32[128,256]{1,0:T(8,128)} async-done(((f32[128,256]{1,0:T(8,128)}), f32[128,256]{1,0:T(8,128)}) %all-reduce.5.cloned.1.call-update) | async-done | bytes 131088 | tf_op jit(solution)/shard_map/psum | solution.py:11
  128.9 1.5 multiply_reduce_fusion.1
  131.1 1.2 convolution_subtract_fusion.5
  132.3 1.1 fusion.25
  133.4 1.0 convolution_subtract_fusion.4
  134.7 1.0 convolution_subtract_fusion.3
  136.0 1.4 fusion.5
  137.5 207.9 %all-reduce.7.cloned.1.call-done = f32[1024,128]{1,0:T(8,128)} async-done(((f32[1024,128]{1,0:T(8,128)}), f32[1024,128]{1,0:T(8,128)}) %all-reduce.7.cloned.1.call-update) | async-done | bytes 524304 | tf_op jit(solution)/shard_map/psum | solution.py:11
  345.5 2.0 fusion.14
  347.5 1.5 fusion.8
  349.0 2.5 copy.10
  351.6 7.3 all-to-all-start
  359.3 29.3 %all-to-all-done = f32[16,128,256]{2,1,0:T(8,128)S(1)} async-done(((f32[16,128,256]{2,1,0:T(8,128)}), f32[16,128,256]{2,1,0:T(8,128)S(1)}, u32[]{:S(2)}, u32[]{:S(2)}) %all-to-all-start) | async-done | bytes 2097184 | tf_op jit(solution)/shard_map/all_to_all | solution.py:82
  388.5 2.2 fusion.2
  393.2 110.5 %all-reduce.9.cloned.1.call-done = f32[128,256]{1,0:T(8,128)} async-done(((f32[128,256]{1,0:T(8,128)}), f32[128,256]{1,0:T(8,128)}) %all-reduce.9.cloned.1.call-update) | async-done | bytes 131088 | tf_op jit(solution)/shard_map/psum | solution.py:11
  503.7 1.5 multiply_reduce_fusion
  505.9 1.2 convolution_subtract_fusion.2
  507.1 1.1 fusion.22
  508.2 1.0 convolution_subtract_fusion.1
  509.5 1.0 convolution_subtract_fusion
  510.8 1.4 fusion.4
  512.3 207.9 %all-reduce.11.cloned.1.call-done = f32[1024,128]{1,0:T(8,128)} async-done(((f32[1024,128]{1,0:T(8,128)}), f32[1024,128]{1,0:T(8,128)}) %all-reduce.11.cloned.1.call-update) | async-done | bytes 524304 | tf_op jit(solution)/shard_map/psum | solution.py:11
  720.3 2.0 fusion.12
  722.3 1.5 fusion.6
  723.8 2.5 copy.14
  726.4 7.3 all-to-all-start.1
  733.9 2.3 pad_maximum_fusion
  736.2 27.2 %all-to-all-done.1 = f32[16,128,256]{2,1,0:T(8,128)S(1)} async-done(((f32[16,128,256]{2,1,0:T(8,128)}), f32[16,128,256]{2,1,0:T(8,128)S(1)}, u32[]{:S(2)}, u32[]{:S(2)}) %all-to-all-start.1) | async-done | bytes 2097184 | tf_op jit(solution)/shard_map/all_to_all | solution.py:82
  763.4 2.2 fusion
  766.0 1.1 bitcast_subtract_fusion
  (60 shorter events, 5.9 us)
Async XLA Ops:
  7.2 1.3 copy-start.4
  7.2 3.1 copy-start.5
  7.2 2.9 copy-start.6
  7.2 3.1 copy-start.7
  7.2 121.7 %all-reduce.5.cloned.1.call-start = ((), (), s32[]{:S(2)}) async-start(), calls=%async_computation.2 | async-start | bytes 262144 | tf_op jit(solution)/shard_map/psum | solution.py:11
  10.1 335.4 %all-reduce.7.cloned.1.call-start = ((), (), s32[]{:S(2)}) async-start(), calls=%async_computation.3 | async-start | bytes 1048576 | tf_op jit(solution)/shard_map/psum | solution.py:11
  128.9 216.6 %copy-start.2 = (f32[128,256]{1,0:T(8,128)S(1)}, f32[128,256]{1,0:T(8,128)}, u32[]{:S(2)}) copy-start(f32[128,256]{1,0:T(8,128)} %all-reduce.5.cloned.1.call-done) | copy-start | bytes 393220
  136.0 213.0 %copy-start = (f32[1024,256]{1,0:T(8,128)}, f32[1024,256]{1,0:T(8,128)S(1)}, u32[]{:S(2)}) copy-start(f32[1024,256]{1,0:T(8,128)S(1)} %select_dynamic-update-slice_fusion.1) | copy-start | bytes 3145732
  351.6 37.0 %all-to-all-start = ((f32[16,128,256]{2,1,0:T(8,128)}), f32[16,128,256]{2,1,0:T(8,128)S(1)}, u32[]{:S(2)}, u32[]{:S(2)}) async-start(f32[16,128,256]{2,1,0:T(8,128)} %copy.10), calls=%async_computation | async-start | bytes 4194304 | tf_op jit(solution)/shard_map/all_to_all | solution.py:82
  358.8 144.9 %all-reduce.9.cloned.1.call-start = ((), (), s32[]{:S(2)}) async-start(), calls=%async_computation.4 | async-start | bytes 262144 | tf_op jit(solution)/shard_map/psum | solution.py:11
  388.5 2.6 copy-start.1
  392.8 327.4 %all-reduce.11.cloned.1.call-start = ((), (), s32[]{:S(2)}) async-start(), calls=%async_computation.5 | async-start | bytes 1048576 | tf_op jit(solution)/shard_map/psum | solution.py:11
  503.7 216.6 %copy-start.3 = (f32[128,256]{1,0:T(8,128)S(1)}, f32[128,256]{1,0:T(8,128)}, u32[]{:S(2)}) copy-start(f32[128,256]{1,0:T(8,128)} %all-reduce.9.cloned.1.call-done) | copy-start | bytes 393220
  726.4 37.0 %all-to-all-start.1 = ((f32[16,128,256]{2,1,0:T(8,128)}), f32[16,128,256]{2,1,0:T(8,128)S(1)}, u32[]{:S(2)}, u32[]{:S(2)}) async-start(f32[16,128,256]{2,1,0:T(8,128)} %copy.14), calls=%async_computation.1 | async-start | bytes 4194304 | tf_op jit(solution)/shard_map/all_to_all | solution.py:82
Sparse Core Ops, SparseCore 0:
  11.8 117.0 all-reduce.4
  137.5 207.9 all-reduce.6
  393.0 110.6 all-reduce.8
  512.3 207.9 all-reduce.10
where the time goes:
time: 774 us
  waiting for transfers between devices  701 us (91%)
  matrix products  24.4 us (3%)
  between operations  15.4 us (2%)
  starting transfers between devices  14.8 us (2%)
  local copies, waits for them, and re-layouts  9.03 us (1%)
  other arithmetic  8.62 us (1%)
    psum x4, waiting for transfers between devices, spread(): return lax.psum(block, axis)  645 us
    all_to_all x2, waiting for transfers between devices, shards(): lax.all_to_all(outgoing, 'prow', split_axis=0, concat_axis=0, tiled=True)  56.4 us
  transfers between devices with their start and end apart: 6, of which 6 were waited for; matrix products, arithmetic and copies ran while one was open for 0% of the time, Pallas kernels for 0%

commit v1 on v0

--- a/solution.py
+++ b/solution.py
@@ -4,11 +4,12 @@
 from jax.sharding import PartitionSpec as P
 
 SWEEPS = 3
+_close_corner = lambda mine_x, axis_key: jnp.sum(jax.lax.all_gather(mine_x, axis_key), axis=0)
 
 
 def spread(block, axis, owner):
     block = jnp.where(lax.axis_index(axis) == owner, block, jnp.zeros_like(block))
-    return lax.psum(block, axis)
+    return _close_corner(block, axis)
 
 
 def refine(pivot_block):

time: 774 us -> 469 us (0.61)
  waiting for transfers between devices: 701 us -> 391 us
  other arithmetic: 8.62 us -> 23.3 us
  matrix products: 24.4 us -> 14.9 us
    psum x4 -> x0, waiting for transfers between devices: 645 us -> none  [spread(): return lax.psum(block, axis)]
    all_gather x0 -> x4, waiting for transfers between devices: none -> 335 us  [jax.lax.all_gather(mine_x, axis_key)]
    reduce_sum x0 -> x4, other arithmetic: none -> 16.6 us  [jnp.sum(jax.lax.all_gather(mine_x, axis_key), axis=0)]
  transfers between devices with their start and end apart: 6 -> 6, of which waited for: 6 -> 6; matrix products, arithmetic and copies ran while one was open for 0% -> 1% of each run, Pallas kernels for 0% -> 0%
where the time goes in v1:
time: 469 us
  waiting for transfers between devices  391 us (83%)
  other arithmetic  23.3 us (5%)
  between operations  15.4 us (3%)
  matrix products  14.9 us (3%)
  starting transfers between devices  14.8 us (3%)
  local copies, waits for them, and re-layouts  9.07 us (2%)
    all_gather x4, waiting for transfers between devices, jax.lax.all_gather(mine_x, axis_key)  335 us
    all_to_all x2, waiting for transfers between devices, shards(): lax.all_to_all(outgoing, 'prow', split_axis=0, concat_axis=0, tiled=True)  56.7 us
    reduce_sum x4, other arithmetic, jnp.sum(jax.lax.all_gather(mine_x, axis_key), axis=0)  16.6 us
    all_to_all x2, starting transfers between devices, shards(): lax.all_to_all(outgoing, 'prow', split_axis=0, concat_axis=0, tiled=True)  14.5 us
  transfers between devices with their start and end apart: 6, of which 6 were waited for; matrix products, arithmetic and copies ran while one was open for 1% of the time, Pallas kernels for 0%

profile of v1, /device:TPU:8, one launch (start us, length us, event | category | flops | bytes accessed | tf_op | source)
XLA Modules:
  0.0 468.9 jit_solution(471122554007233472)
XLA Ops:
  7.2 1.2 copy.34
  8.5 0.8 gather_fusion
  9.3 0.7 select_select_fusion.1
  10.3 65.7 %all-gather.9.cloned.1.call-done = f32[2048,256]{1,0:T(8,128)} async-done(((f32[128,256]{1,0:T(8,128)}), f32[2048,256]{1,0:T(8,128)}) %all-gather.9.cloned.1.call-update) | async-done | bytes 2097168 | tf_op jit(solution)/shard_map/all_gather | solution.py:7
  75.9 1.7 reduce_sum.54
  77.7 0.6 multiply_reduce_fusion.1
  80.4 1.4 fusion.5
  82.1 106.5 %all-gather.11.cloned.1.call-done = f32[32768,128]{1,0:T(8,128)} async-done(((f32[1024,128]{1,0:T(8,128)}), f32[32768,128]{1,0:T(8,128)}) %all-gather.11.cloned.1.call-update) | async-done | bytes 16777232 | tf_op jit(solution)/shard_map/all_gather | solution.py:7
  188.5 6.6 %reduce_sum.56 = f32[1024,128]{1,0:T(8,128)S(1)} reduce(f32[32,1024,128]{2,1,0:T(8,128)} %bitcast.92, f32[]{:T(128)} %constant.132.clone.1), dimensions={0}, to_apply=%region_2.4 | reduce | flops 4063232 | bytes 17301508 | tf_op jit(solution)/shard_map/reduce_sum | solution.py:7
  195.1 1.1 fusion.10
  196.2 1.1 fusion.46
  197.4 2.6 copy.10
  199.9 7.3 %all-to-all-start = ((f32[16,128,256]{2,1,0:T(8,128)}), f32[16,128,256]{2,1,0:T(8,128)S(1)}, u32[]{:S(2)}, u32[]{:S(2)}) async-start(f32[16,128,256]{2,1,0:T(8,128)} %copy.10), calls=%async_computation | async-start | bytes 4194304 | tf_op jit(solution)/shard_map/all_to_all | solution.py:83
  207.6 29.5 %all-to-all-done = f32[16,128,256]{2,1,0:T(8,128)S(1)} async-done(((f32[16,128,256]{2,1,0:T(8,128)}), f32[16,128,256]{2,1,0:T(8,128)S(1)}, u32[]{:S(2)}, u32[]{:S(2)}) %all-to-all-start) | async-done | bytes 2097184 | tf_op jit(solution)/shard_map/all_to_all | solution.py:83
  237.0 2.2 fusion.2
  239.3 0.3 copy.12
  239.8 0.8 gather_fusion.1
  240.6 0.7 select_select_fusion
  241.7 55.9 %all-gather.13.cloned.1.call-done = f32[2048,256]{1,0:T(8,128)} async-done(((f32[128,256]{1,0:T(8,128)}), f32[2048,256]{1,0:T(8,128)}) %all-gather.13.cloned.1.call-update) | async-done | bytes 2097168 | tf_op jit(solution)/shard_map/all_gather | solution.py:7
  297.6 1.7 reduce_sum.57
  299.3 0.6 multiply_reduce_fusion
  302.0 1.4 fusion.4
  303.6 106.6 %all-gather.15.cloned.1.call-done = f32[32768,128]{1,0:T(8,128)} async-done(((f32[1024,128]{1,0:T(8,128)}), f32[32768,128]{1,0:T(8,128)}) %all-gather.15.cloned.1.call-update) | async-done | bytes 16777232 | tf_op jit(solution)/shard_map/all_gather | solution.py:7
  410.1 6.6 %reduce_sum.59 = f32[1024,128]{1,0:T(8,128)S(1)} reduce(f32[32,1024,128]{2,1,0:T(8,128)} %bitcast.93, f32[]{:T(128)} %constant.132.clone.1), dimensions={0}, to_apply=%region_5.7 | reduce | flops 4063232 | bytes 17301508 | tf_op jit(solution)/shard_map/reduce_sum | solution.py:7
  416.7 1.1 fusion.8
  417.8 1.1 fusion.50
  419.0 2.6 copy.14
  421.5 7.3 %all-to-all-start.1 = ((f32[16,128,256]{2,1,0:T(8,128)}), f32[16,128,256]{2,1,0:T(8,128)S(1)}, u32[]{:S(2)}, u32[]{:S(2)}) async-start(f32[16,128,256]{2,1,0:T(8,128)} %copy.14), calls=%async_computation.1 | async-start | bytes 4194304 | tf_op jit(solution)/shard_map/all_to_all | solution.py:83
  429.1 2.3 pad_maximum_fusion
  431.4 27.3 %all-to-all-done.1 = f32[16,128,256]{2,1,0:T(8,128)S(1)} async-done(((f32[16,128,256]{2,1,0:T(8,128)}), f32[16,128,256]{2,1,0:T(8,128)S(1)}, u32[]{:S(2)}, u32[]{:S(2)}) %all-to-all-start.1) | async-done | bytes 2097184 | tf_op jit(solution)/shard_map/all_to_all | solution.py:83
  458.6 2.2 fusion
  461.2 1.1 bitcast_subtract_fusion
  (63 shorter events, 5.2 us)
Async XLA Ops:
  7.2 1.3 copy-start.4
  7.2 2.9 copy-start.6
  7.2 68.7 %all-gather.9.cloned.1.call-start = ((), (), s32[]{:S(2)}) async-start(), calls=%async_computation.2 | async-start | bytes 2228224 | tf_op jit(solution)/shard_map/all_gather | solution.py:7
  10.0 178.5 %all-gather.11.cloned.1.call-start = ((), (), s32[]{:S(2)}) async-start(), calls=%async_computation.3 | async-start | bytes 17301504 | tf_op jit(solution)/shard_map/all_gather | solution.py:7
  77.7 4.2 copy-start.7
  77.7 4.3 copy-start.5
  78.3 116.8 %copy-start = (f32[1024,256]{1,0:T(8,128)}, f32[1024,256]{1,0:T(8,128)S(1)}, u32[]{:S(2)}) copy-start(f32[1024,256]{1,0:T(8,128)S(1)} %select_dynamic-update-slice_fusion.1) | copy-start | bytes 3145732
  195.1 2.2 copy-start.2
  199.9 37.1 %all-to-all-start = ((f32[16,128,256]{2,1,0:T(8,128)}), f32[16,128,256]{2,1,0:T(8,128)S(1)}, u32[]{:S(2)}, u32[]{:S(2)}) async-start(f32[16,128,256]{2,1,0:T(8,128)} %copy.10), calls=%async_computation | async-start | bytes 4194304 | tf_op jit(solution)/shard_map/all_to_all | solution.py:83
  207.2 90.4 %all-gather.13.cloned.1.call-start = ((), (), s32[]{:S(2)}) async-start(), calls=%async_computation.4 | async-start | bytes 2228224 | tf_op jit(solution)/shard_map/all_gather | solution.py:7
  237.0 2.6 copy-start.1
  241.3 168.8 %all-gather.15.cloned.1.call-start = ((), (), s32[]{:S(2)}) async-start(), calls=%async_computation.5 | async-start | bytes 17301504 | tf_op jit(solution)/shard_map/all_gather | solution.py:7
  416.7 2.2 copy-start.3
  421.5 37.1 %all-to-all-start.1 = ((f32[16,128,256]{2,1,0:T(8,128)}), f32[16,128,256]{2,1,0:T(8,128)S(1)}, u32[]{:S(2)}, u32[]{:S(2)}) async-start(f32[16,128,256]{2,1,0:T(8,128)} %copy.14), calls=%async_computation.1 | async-start | bytes 4194304 | tf_op jit(solution)/shard_map/all_to_all | solution.py:83
Sparse Core Ops, SparseCore 0:
  11.6 64.2 all-gather.8
  81.9 106.5 all-gather.10
  241.5 56.0 all-gather.12
  303.5 106.5 all-gather.14
